TPU v7x, 512 devices: a whole 4x4x16 slice. The times are simulated.
512 devices in a mesh: face: 4 (over z_lo), tile: 64 (over y, z_hi, x), lev: 2 (over core).
Axes of the slice: x: 4, y: 4, z: 16 (z_hi: 4, z_lo: 4; z = z_hi * 4 + z_lo), core: 2. Of those that a mesh axis runs over, the one named last changes fastest.
Arguments:
- flux: float32 [2048, 8, 512], P(('face', 'tile')), may hold values from -6 to 6
- profile: float32 [16], P('lev'), may hold values from 0.2 to 1
- courant: float32 [2, 16, 512, 2048], P(None, 'lev', 'tile', 'face'), may hold values from 0.05 to 0.45
- winds: int32 [2, 16, 512, 2048], P(None, 'lev', 'tile', 'face'), may hold values from 0 to 1
- cells: int32 [64, 4, 128], P('tile', 'face'), may hold values from 0 to 4095, as said below
- counts: int32 [64, 4], P('tile', 'face'), may hold values from 32 to 128, as said below
- kernels: float32 [16, 64, 4, 128], P('lev', 'tile', 'face'), may hold values from 0.25 to 0.75
- month_weight: float32 [8, 64, 4, 128], P(None, 'tile', 'face'), may hold values from 0 to 1
- observed: float32 [64, 4, 128], P('tile', 'face'), may hold values from -8 to 8
- obs_weight: float32 [64, 4, 128], P('tile', 'face'), may hold values from 0.5 to 2
- precision: float32 [8], replicated, may hold values from 0.5 to 2
Outputs:
- flux_gradient: float32 [8, 512, 2048], P(None, 'tile', 'face')
- precision_gradient: float32 [8], replicated
Inputs may be any that keep to these rules, and one draw needn't show every extreme that they name: Within each block the 128 entries are distinct cells, numbered row by row over the block's 8 rows of 512 cells; the first four slots of every block hold, in some order, a cell of the block's first column, one of its last column, and interior cells of its first row and of its last row. `counts`: slot s of a block holds a sounding when s is below the block's count; some block is full and some holds exactly 32.
All inputs are finite; a program needn't handle non-finite values.
Results may differ from a plain program's by a relative error of at most 0.00015.
Values sent between devices are 32-bit elements; how exact they have to be, the bound alone decides.
A program may use at most 64 MiB of HBM per device.

v0:
```python
import jax
import jax.numpy as jnp
from jax import lax
from jax.sharding import PartitionSpec as P

KAPPA = 0.025


def extended(x, sides, width, wrap):
    for axis, dim in sides:
        devices, length = (lax.axis_size(axis), x.shape[dim])
        up = [(i, (i + 1) % devices) for i in range(devices if wrap else devices - 1)]
        down = [(j, i) for i, j in up]
        last = lax.slice_in_dim(x, length - width, length, axis=dim)
        initial = lax.slice_in_dim(x, 0, width, axis=dim)
        before = lax.ppermute(last, axis, up)
        after = lax.ppermute(initial, axis, down)
        x = jnp.concatenate([before, x, after], axis=dim)
    return x


def shifted(x, axis, by):
    devices = lax.axis_size(axis)
    return lax.ppermute(x, axis, [(i, (i + by) % devices) for i in range(devices)])


def shifted_2(value, axis, steps):
    count = lax.axis_size(axis)
    initial, last = (max(0, -steps), min(count, count - steps))
    return lax.ppermute(value, axis, [(source, source + steps) for source in range(initial, last)])


def weights_from(speed_x, speed_y, east_flag, north_flag):
    w_west = speed_x * (1.0 - east_flag) + KAPPA
    w_east = speed_x * east_flag + KAPPA
    w_south = speed_y * (1.0 - north_flag) + KAPPA
    w_north = speed_y * north_flag + KAPPA
    w_centre = 1.0 - speed_x - speed_y - 4.0 * KAPPA
    return (w_centre, w_west, w_east, w_south, w_north)


def flags_of(winds):
    return ((winds[0] == 1).astype(jnp.float32), (winds[1] == 1).astype(jnp.float32))


def advance(conc, coeffs):
    w_centre, w_west, w_east, w_south, w_north = coeffs
    side = extended(conc, (("face", 3),), 1, True)
    rim = extended(conc, (("tile", 2),), 1, False)
    return (
        w_centre * conc
        + w_west * side[..., :-2]
        + w_east * side[..., 2:]
        + w_south * rim[..., :-2, :]
        + w_north * rim[..., 2:, :]
    )


def retreat(grad, coeffs):
    w_centre, w_west, w_east, w_south, w_north = coeffs
    west_weighted = w_west * grad
    east_weighted = w_east * grad
    south_weighted = w_south * grad
    north_weighted = w_north * grad
    from_east = shifted(west_weighted[..., :1], "face", -1)
    from_west = shifted(east_weighted[..., -1:], "face", 1)
    from_above = shifted_2(south_weighted[..., :1, :], "tile", -1)
    from_below = shifted_2(north_weighted[..., -1:, :], "tile", 1)
    west_part = jnp.concatenate([west_weighted[..., 1:], from_east], -1)
    east_part = jnp.concatenate([from_west, east_weighted[..., :-1]], -1)
    south_part = jnp.concatenate([south_weighted[..., 1:, :], from_above], -2)
    north_part = jnp.concatenate([from_below, north_weighted[..., :-1, :]], -2)
    return w_centre * grad + west_part + east_part + south_part + north_part


def on_device(
    flux,
    profile,
    courant,
    winds,
    cells,
    counts,
    kernels,
    month_weight,
    observed,
    obs_weight,
    precision,
):
    n_tracer = flux.shape[1]
    n_level = profile.shape[0]
    slot_total = cells.shape[2]
    moved = lax.all_to_all(flux, "tile", split_axis=2, concat_axis=0, tiled=True)
    field = jnp.transpose(moved, (1, 2, 0))
    rows_dev = field.shape[1]
    cols_dev = field.shape[2]
    n_cell = rows_dev * cols_dev
    east_flag, north_flag = flags_of(winds)
    conc = profile[None, :, None, None] * field[:, None]
    coeffs = weights_from(courant[0], courant[1], east_flag, north_flag)
    conc = advance(advance(conc, coeffs), coeffs)
    slot_cells = cells.reshape(slot_total)
    live = jnp.arange(slot_total, dtype=jnp.int32) < counts.reshape(())
    picker = jnp.where(
        live[:, None] & (slot_cells[:, None] == jnp.arange(n_cell, dtype=jnp.int32)[None, :]),
        1.0,
        0.0,
    ).astype(jnp.float32)
    flat = conc.reshape(n_tracer, n_level, n_cell)
    sampled = jnp.einsum("tlc,sc->tls", flat, picker, precision=lax.Precision.HIGHEST)
    kern = kernels.reshape(n_level, slot_total)
    monthly = month_weight.reshape(n_tracer, slot_total)
    partial_model = jnp.sum(kern * jnp.sum(monthly[:, None, :] * sampled, 0), 0)
    model = lax.psum(partial_model, "lev")
    forcing = jnp.where(
        live, obs_weight.reshape(slot_total) * (observed.reshape(slot_total) - model), 0.0
    )
    values = kern[None] * (monthly * forcing[None])[:, None, :]
    lam = jnp.einsum("tls,sc->tlc", values, picker, precision=lax.Precision.HIGHEST)
    lam = lam.reshape(n_tracer, n_level, rows_dev, cols_dev)
    lam = retreat(retreat(lam, coeffs), coeffs)
    adj_part = jnp.sum(profile[None, :, None, None] * lam, 1)
    all_cells = n_cell * lax.axis_size("tile") * lax.axis_size("face")
    adj = lax.psum(adj_part, "lev")
    flux_gradient = precision[:, None, None] * field - adj
    square_sum = lax.psum(jnp.sum(adj * adj, axis=(1, 2)), ("face", "tile"))
    precision_gradient = 0.5 / precision - 0.5 * (square_sum / all_cells) / (precision * precision)
    return (flux_gradient, precision_gradient)


def solution(mesh):
    return jax.shard_map(
        on_device,
        mesh=mesh,
        in_specs=(
            P(("face", "tile"), None, None),
            P("lev"),
            P(None, "lev", "tile", "face"),
            P(None, "lev", "tile", "face"),
            P("tile", "face", None),
            P("tile", "face"),
            P("lev", "tile", "face", None),
            P(None, "tile", "face", None),
            P("tile", "face", None),
            P("tile", "face", None),
            P(),
        ),
        out_specs=(P(None, "tile", "face"), P()),
        check_vma=False,
    )
```

profile of v0, /device:TPU:32, one launch (start us, length us, event | category | flops | bytes accessed | tf_op | source)
XLA Modules:
  0.0 1168.7 jit_solution(5610475102505204907)
XLA Ops:
  7.2 1.7 copy.25
  8.9 1.7 reshape.69
  10.6 20.3 %all-to-all-start = ((f32[64,1,512]{2,1,0:T(1,128)}), f32[64,1,512]{2,1,0:T(1,128)S(1)}, u32[]{:S(2)}, u32[]{:S(2)}) async-start(f32[64,1,512]{2,1,0:T(1,128)} %reshape.69), calls=%async_computation | async-start | bytes 262144 | tf_op jit(solution)/shard_map/all_to_all | solution.py:92
  31.1 20.0 %all-to-all-done = f32[64,1,512]{2,1,0:T(1,128)S(1)} async-done(((f32[64,1,512]{2,1,0:T(1,128)}), f32[64,1,512]{2,1,0:T(1,128)S(1)}, u32[]{:S(2)}, u32[]{:S(2)}) %all-to-all-start) | async-done | bytes 131104 | tf_op jit(solution)/shard_map/all_to_all | solution.py:92
  53.7 2.4 copy.27
  56.1 2.8 all_to_all.16
  59.3 2.5 collective-permute-start.2
  61.8 1.3 collective-permute-start.3
  63.1 2.9 collective-permute-start
  66.1 2.9 collective-permute-start.1
  70.1 4.1 collective-permute-done
  74.2 7.7 collective-permute-done.1
  82.7 1.3 collective-permute-start.6
  85.5 5.5 collective-permute-start.4
  91.0 1.9 collective-permute-start.5
  93.0 7.6 collective-permute-done.4
  101.3 2.4 fusion.12
  103.8 2.6 psum.21
  106.5 1.7 fusion
  110.1 4.9 collective-permute-start.11
  115.2 3.2 collective-permute-start.8
  118.4 3.1 collective-permute-start.9
  122.2 3.8 collective-permute-done.8
  126.0 6.6 collective-permute-done.9
  133.6 4.2 collective-permute-start.12
  138.6 5.9 collective-permute-start.15
  146.0 3.7 collective-permute-start.13
  149.8 7.5 collective-permute-done.13
  157.8 9.1 collective-permute-done.14
  168.8 66.5 %all-reduce.2.cloned.1.call-done = f32[8,8,512]{2,1,0:T(8,128)} async-done(((f32[8,8,512]{2,1,0:T(8,128)}), f32[8,8,512]{2,1,0:T(8,128)}) %all-reduce.2.cloned.1.call-update) | async-done | bytes 131088 | tf_op jit(solution)/shard_map/psum | solution.py:123
  235.3 1.7 multiply_reduce_fusion.1
  237.0 924.4 %psum.23 = f32[8]{0:T(128)S(1)} all-reduce(f32[8]{0:T(128)S(1)} %get-tuple-element.33), channel_id=1, replica_groups=mesh['face'=4,'tile'=64,'lev'=2] {'face','tile'}, use_global_device_ids=true, to_apply=%region_6.7 | all-reduce | flops 8 | bytes 64 | tf_op jit(solution)/shard_map/psum | solution.py:125
  (78 shorter events, 15.5 us)
Async XLA Ops:
  7.2 23.8 %copy-start = (f32[2,8,8,512]{3,2,1,0:T(8,128)S(1)}, f32[2,8,8,512]{3,2,1,0:T(8,128)}, u32[]{:S(2)}) copy-start(f32[2,8,8,512]{3,2,1,0:T(8,128)} %param.13) | copy-start | bytes 786436
  7.2 23.8 %copy-start.1 = (s32[2,8,8,512]{3,2,1,0:T(8,128)S(1)}, s32[2,8,8,512]{3,2,1,0:T(8,128)}, u32[]{:S(2)}) copy-start(s32[2,8,8,512]{3,2,1,0:T(8,128)} %param.14) | copy-start | bytes 786436
  10.6 40.5 %all-to-all-start = ((f32[64,1,512]{2,1,0:T(1,128)}), f32[64,1,512]{2,1,0:T(1,128)S(1)}, u32[]{:S(2)}, u32[]{:S(2)}) async-start(f32[64,1,512]{2,1,0:T(1,128)} %reshape.69), calls=%async_computation | async-start | bytes 262144 | tf_op jit(solution)/shard_map/all_to_all | solution.py:92
  30.9 204.3 %all-reduce.2.cloned.1.call-start = ((), (), s32[]{:S(2)}) async-start(), calls=%async_computation.1 | async-start | bytes 262144 | tf_op jit(solution)/shard_map/psum | solution.py:123
  56.1 2.8 copy-start.4
  59.3 22.6 %collective-permute-start.2 = (f32[8,8,1,512]{3,1,2,0:T(8,128)S(1)}, f32[8,8,1,512]{3,1,2,0:T(8,128)S(1)}, u32[]{:S(2)}, u32[]{:S(2)}) collective-permute-start(f32[8,8,1,512]{3,1,2,0:T(8,128)S(1)} %get-tuple-element.25), channel_id=1, source_target_pairs={{0,2},{2,4},{4,6},{6,8},{8,10},{10,12},{12,14},{14,16},{16,18},{18... | collective-permute-start | bytes 393224 | tf_op jit(solution)/shard_map/ppermute | solution.py:16
  61.8 20.1 %collective-permute-start.3 = (f32[8,8,1,512]{3,1,2,0:T(8,128)S(1)}, f32[8,8,1,512]{3,1,2,0:T(8,128)S(1)}, u32[]{:S(2)}, u32[]{:S(2)}) collective-permute-start(f32[8,8,1,512]{3,1,2,0:T(8,128)S(1)} %get-tuple-element.26), channel_id=1, source_target_pairs={{2,0},{4,2},{6,4},{8,6},{10,8},{12,10},{14,12},{16,14},{18,16},{20... | collective-permute-start | bytes 393224 | tf_op jit(solution)/shard_map/ppermute | solution.py:17
  63.1 11.1 collective-permute-start
  66.1 15.9 %collective-permute-start.1 = (f32[8,8,8,1]{3,1,2,0:T(8,128)S(1)}, f32[8,8,8,1]{3,1,2,0:T(8,128)S(1)}, u32[]{:S(2)}, u32[]{:S(2)}) collective-permute-start(f32[8,8,8,1]{3,1,2,0:T(8,128)S(1)} %get-tuple-element.24), channel_id=1, source_target_pairs={{128,0},{256,128},{384,256},{0,384},{129,1},{257,129},{385,257},{1... | collective-permute-start | bytes 6152 | tf_op jit(solution)/shard_map/ppermute | solution.py:17
  82.7 17.8 %collective-permute-start.6 = (f32[8,8,1,512]{3,1,2,0:T(8,128)S(1)}, f32[8,8,1,512]{3,1,2,0:T(8,128)S(1)}, u32[]{:S(2)}, u32[]{:S(2)}) collective-permute-start(f32[8,8,1,512]{3,1,2,0:T(8,128)S(1)} %get-tuple-element.21), channel_id=1, source_target_pairs={{0,2},{2,4},{4,6},{6,8},{8,10},{10,12},{12,14},{14,16},{16,18},{18... | collective-permute-start | bytes 393224 | tf_op jit(solution)/shard_map/ppermute | solution.py:16
  84.0 17.3 %copy-start.2 = (f32[8,1,1,128]{3,2,1,0:T(1,128)S(1)}, f32[8,1,1,128]{3,2,1,0:T(1,128)}, u32[]{:S(2)}) copy-start(f32[8,1,1,128]{3,2,1,0:T(1,128)} %param.18) | copy-start | bytes 12292
  84.0 17.3 %copy-start.8 = (s32[1,1,128]{2,1,0:T(1,128)S(1)}, s32[1,1,128]{2,1,0:T(1,128)}, u32[]{:S(2)}) copy-start(s32[1,1,128]{2,1,0:T(1,128)} %param.15) | copy-start | bytes 1540
  84.0 16.5 %collective-permute-start.7 = (f32[8,8,1,512]{3,1,2,0:T(8,128)S(1)}, f32[8,8,1,512]{3,1,2,0:T(8,128)S(1)}, u32[]{:S(2)}, u32[]{:S(2)}) collective-permute-start(f32[8,8,1,512]{3,1,2,0:T(8,128)S(1)} %get-tuple-element.22), channel_id=1, source_target_pairs={{2,0},{4,2},{6,4},{8,6},{10,8},{12,10},{14,12},{16,14},{18,16},{20... | collective-permute-start | bytes 393224 | tf_op jit(solution)/shard_map/ppermute | solution.py:17
  85.5 15.0 %collective-permute-start.4 = (f32[8,8,8,1]{3,1,2,0:T(8,128)S(1)}, f32[8,8,8,1]{3,1,2,0:T(8,128)S(1)}, u32[]{:S(2)}, u32[]{:S(2)}) collective-permute-start(f32[8,8,8,1]{3,1,2,0:T(8,128)S(1)} %get-tuple-element.19), channel_id=1, source_target_pairs={{0,128},{128,256},{256,384},{384,0},{1,129},{129,257},{257,385},{3... | collective-permute-start | bytes 6152 | tf_op jit(solution)/shard_map/ppermute | solution.py:16
  91.0 9.6 collective-permute-start.5
  92.9 10.9 copy-start.3
  92.9 13.5 %copy-start.6 = (f32[1,1,128]{2,1,0:T(1,128)S(1)}, f32[1,1,128]{2,1,0:T(1,128)}, u32[]{:S(2)}) copy-start(f32[1,1,128]{2,1,0:T(1,128)} %param.19) | copy-start | bytes 1540
  92.9 13.5 %copy-start.7 = (f32[1,1,128]{2,1,0:T(1,128)S(1)}, f32[1,1,128]{2,1,0:T(1,128)}, u32[]{:S(2)}) copy-start(f32[1,1,128]{2,1,0:T(1,128)} %param.20) | copy-start | bytes 1540
  108.8 23.7 %collective-permute-start.10 = (f32[8,8,1,512]{3,1,2,0:T(8,128)S(1)}, f32[8,8,1,512]{3,1,2,0:T(8,128)S(1)}, u32[]{:S(2)}, u32[]{:S(2)}) collective-permute-start(f32[8,8,1,512]{3,1,2,0:T(8,128)S(1)} %slice.165), channel_id=1, source_target_pairs={{2,0},{4,2},{6,4},{8,6},{10,8},{12,10},{14,12},{16,14},{18,16},{20... | collective-permute-start | bytes 393224 | tf_op jit(solution)/shard_map/ppermute | solution.py:30
  110.1 22.4 %collective-permute-start.11 = (f32[8,8,1,512]{3,1,2,0:T(8,128)S(1)}, f32[8,8,1,512]{3,1,2,0:T(8,128)S(1)}, u32[]{:S(2)}, u32[]{:S(2)}) collective-permute-start(f32[8,8,1,512]{3,1,2,0:T(8,128)S(1)} %slice.166), channel_id=1, source_target_pairs={{0,2},{2,4},{4,6},{6,8},{8,10},{10,12},{12,14},{14,16},{16,18},{18... | collective-permute-start | bytes 393224 | tf_op jit(solution)/shard_map/ppermute | solution.py:30
  115.2 10.7 collective-permute-start.8
  118.4 14.1 %collective-permute-start.9 = (f32[8,8,8,1]{3,1,2,0:T(8,128)S(1)}, f32[8,8,8,1]{3,1,2,0:T(8,128)S(1)}, u32[]{:S(2)}, u32[]{:S(2)}) collective-permute-start(f32[8,8,8,1]{3,1,2,0:T(8,128)S(1)} %slice.162), channel_id=1, source_target_pairs={{0,128},{128,256},{256,384},{384,0},{1,129},{129,257},{257,385},{3... | collective-permute-start | bytes 6152 | tf_op jit(solution)/shard_map/ppermute | solution.py:24
  133.6 16.0 %collective-permute-start.12 = (f32[8,8,8,1]{3,1,2,0:T(8,128)S(1)}, f32[8,8,8,1]{3,1,2,0:T(8,128)S(1)}, u32[]{:S(2)}, u32[]{:S(2)}) collective-permute-start(f32[8,8,8,1]{3,1,2,0:T(8,128)S(1)} %slice.169), channel_id=1, source_target_pairs={{0,384},{128,0},{256,128},{384,256},{1,385},{129,1},{257,129},{385... | collective-permute-start | bytes 6152 | tf_op jit(solution)/shard_map/ppermute | solution.py:24
  138.6 19.1 %collective-permute-start.15 = (f32[8,8,1,512]{3,1,2,0:T(8,128)S(1)}, f32[8,8,1,512]{3,1,2,0:T(8,128)S(1)}, u32[]{:S(2)}, u32[]{:S(2)}) collective-permute-start(f32[8,8,1,512]{3,1,2,0:T(8,128)S(1)} %slice.174), channel_id=1, source_target_pairs={{0,2},{2,4},{4,6},{6,8},{8,10},{10,12},{12,14},{14,16},{16,18},{18... | collective-permute-start | bytes 393224 | tf_op jit(solution)/shard_map/ppermute | solution.py:30
  144.5 22.3 %collective-permute-start.14 = (f32[8,8,1,512]{3,1,2,0:T(8,128)S(1)}, f32[8,8,1,512]{3,1,2,0:T(8,128)S(1)}, u32[]{:S(2)}, u32[]{:S(2)}) collective-permute-start(f32[8,8,1,512]{3,1,2,0:T(8,128)S(1)} %slice.173), channel_id=1, source_target_pairs={{2,0},{4,2},{6,4},{8,6},{10,8},{12,10},{14,12},{16,14},{18,16},{20... | collective-permute-start | bytes 393224 | tf_op jit(solution)/shard_map/ppermute | solution.py:30
  146.0 11.4 collective-permute-start.13
  166.9 68.3 %copy-start.5 = (f32[8]{0:T(128)S(1)}, f32[8]{0:T(128)}, u32[]{:S(2)}) copy-start(f32[8]{0:T(128)} %param.21) | copy-start | bytes 100
Sparse Core Ops, SparseCore 0:
  169.0 66.2 all-reduce.1
where the time goes:
time: 1170 us
  blocking collectives  927 us (79%)
  waiting for transfers between devices  133 us (11%)
  starting transfers between devices  67.6 us (6%)
  between operations  15.2 us (1%)
  local copies, waits for them, and re-layouts  13.2 us (1%)
    psum x1, blocking collectives, on_device(): square_sum = lax.psum(jnp.sum(adj * adj, axis=(1, 2)), ('face', 'tile'))  924 us
    psum x1, waiting for transfers between devices, on_device(): adj = lax.psum(adj_part, 'lev')  66.5 us
  transfers between devices with their start and end apart: 18, of which 9 were waited for; matrix products, arithmetic and copies ran while one was open for 0% of the time, Pallas kernels for 0%

commit v1 on v0

--- a/solution.py
+++ b/solution.py
@@ -2,6 +2,7 @@
 import jax.numpy as jnp
 from jax import lax
 from jax.sharding import PartitionSpec as P
+from jax.lax import all_gather
 
 KAPPA = 0.025
 
@@ -120,7 +121,8 @@
     lam = retreat(retreat(lam, coeffs), coeffs)
     adj_part = jnp.sum(profile[None, :, None, None] * lam, 1)
     all_cells = n_cell * lax.axis_size("tile") * lax.axis_size("face")
-    adj = lax.psum(adj_part, "lev")
+    piece_next = all_gather(adj_part, "lev")
+    adj = jnp.sum(piece_next, 0)
     flux_gradient = precision[:, None, None] * field - adj
     square_sum = lax.psum(jnp.sum(adj * adj, axis=(1, 2)), ("face", "tile"))
     precision_gradient = 0.5 / precision - 0.5 * (square_sum / all_cells) / (precision * precision)

time: 1170 us -> 1100 us (0.940)
  the two profiles are of different devices: /device:TPU:32 before, /device:TPU:64 now
where the time goes in v1:
time: 1100 us
  blocking collectives  945 us (86%)
  waiting for transfers between devices  65.2 us (6%)
  starting transfers between devices  64.7 us (6%)
  local copies, waits for them, and re-layouts  12.6 us (1%)
    psum x1, blocking collectives, on_device(): square_sum = lax.psum(jnp.sum(adj * adj, axis=(1, 2)), ('face', 'tile'))  941 us
  transfers between devices with their start and end apart: 17, of which 9 were waited for; matrix products, arithmetic and copies ran while one was open for 0% of the time, Pallas kernels for 0%

profile of v1, /device:TPU:64, one launch (start us, length us, event | category | flops | bytes accessed | tf_op | source)
XLA Modules:
  0.0 1101.2 jit_solution(3678466900896953638)
XLA Ops:
  0.6 1.7 copy.25
  2.4 1.7 reshape.70
  4.1 19.4 %all-to-all-start = ((f32[64,1,512]{2,1,0:T(1,128)}), f32[64,1,512]{2,1,0:T(1,128)S(1)}, u32[]{:S(2)}, u32[]{:S(2)}) async-start(f32[64,1,512]{2,1,0:T(1,128)} %reshape.70), calls=%async_computation | async-start | bytes 262144 | tf_op jit(solution)/shard_map/all_to_all | solution.py:93
  23.6 20.1 %all-to-all-done = f32[64,1,512]{2,1,0:T(1,128)S(1)} async-done(((f32[64,1,512]{2,1,0:T(1,128)}), f32[64,1,512]{2,1,0:T(1,128)S(1)}, u32[]{:S(2)}, u32[]{:S(2)}) %all-to-all-start) | async-done | bytes 131104 | tf_op jit(solution)/shard_map/all_to_all | solution.py:93
  46.3 2.4 copy.27
  48.7 2.8 all_to_all.16
  51.8 2.5 collective-permute-start.2
  54.4 1.3 collective-permute-start.3
  55.7 1.9 collective-permute-start
  57.6 3.9 collective-permute-start.1
  62.7 3.6 collective-permute-done
  66.3 10.7 collective-permute-done.1
  77.8 1.3 collective-permute-start.6
  80.6 1.9 collective-permute-start.4
  82.5 3.9 collective-permute-start.5
  86.5 8.0 collective-permute-done.4
  95.3 2.4 fusion.12
  97.8 2.6 psum.14
  100.5 1.7 fusion
  103.9 4.9 collective-permute-start.11
  109.0 1.9 collective-permute-start.8
  110.9 3.9 collective-permute-start.9
  115.4 4.9 collective-permute-done.8
  120.3 4.9 collective-permute-done.9
  126.3 2.5 collective-permute-start.12
  129.7 8.0 collective-permute-start.15
  139.1 3.3 collective-permute-start.13
  142.5 2.4 collective-permute-done.12
  145.0 3.4 collective-permute-done.13
  148.8 7.2 collective-permute-done.14
  157.4 2.0 all_gather.7
  160.2 940.6 %psum.15 = f32[8]{0:T(128)S(1)} all-reduce(f32[8]{0:T(128)S(1)} %get-tuple-element.33), channel_id=1, replica_groups=mesh['face'=4,'tile'=64,'lev'=2] {'face','tile'}, use_global_device_ids=true, to_apply=%region_6.7 | all-reduce | flops 8 | bytes 64 | tf_op jit(solution)/shard_map/psum | solution.py:127
  (77 shorter events, 15.4 us)
Async XLA Ops:
  0.6 22.9 %copy-start = (f32[2,8,8,512]{3,2,1,0:T(8,128)S(1)}, f32[2,8,8,512]{3,2,1,0:T(8,128)}, u32[]{:S(2)}) copy-start(f32[2,8,8,512]{3,2,1,0:T(8,128)} %param.13) | copy-start | bytes 786436
  0.6 22.9 %copy-start.1 = (s32[2,8,8,512]{3,2,1,0:T(8,128)S(1)}, s32[2,8,8,512]{3,2,1,0:T(8,128)}, u32[]{:S(2)}) copy-start(s32[2,8,8,512]{3,2,1,0:T(8,128)} %param.14) | copy-start | bytes 786436
  4.1 39.6 %all-to-all-start = ((f32[64,1,512]{2,1,0:T(1,128)}), f32[64,1,512]{2,1,0:T(1,128)S(1)}, u32[]{:S(2)}, u32[]{:S(2)}) async-start(f32[64,1,512]{2,1,0:T(1,128)} %reshape.70), calls=%async_computation | async-start | bytes 262144 | tf_op jit(solution)/shard_map/all_to_all | solution.py:93
  48.7 2.8 copy-start.4
  51.8 25.2 %collective-permute-start.2 = (f32[8,8,1,512]{3,1,2,0:T(8,128)S(1)}, f32[8,8,1,512]{3,1,2,0:T(8,128)S(1)}, u32[]{:S(2)}, u32[]{:S(2)}) collective-permute-start(f32[8,8,1,512]{3,1,2,0:T(8,128)S(1)} %get-tuple-element.25), channel_id=1, source_target_pairs={{0,2},{2,4},{4,6},{6,8},{8,10},{10,12},{12,14},{14,16},{16,18},{18... | collective-permute-start | bytes 393224 | tf_op jit(solution)/shard_map/ppermute | solution.py:17
  54.4 22.7 %collective-permute-start.3 = (f32[8,8,1,512]{3,1,2,0:T(8,128)S(1)}, f32[8,8,1,512]{3,1,2,0:T(8,128)S(1)}, u32[]{:S(2)}, u32[]{:S(2)}) collective-permute-start(f32[8,8,1,512]{3,1,2,0:T(8,128)S(1)} %get-tuple-element.26), channel_id=1, source_target_pairs={{2,0},{4,2},{6,4},{8,6},{10,8},{12,10},{14,12},{16,14},{18,16},{20... | collective-permute-start | bytes 393224 | tf_op jit(solution)/shard_map/ppermute | solution.py:18
  55.7 10.6 collective-permute-start
  57.6 19.4 %collective-permute-start.1 = (f32[8,8,8,1]{3,1,2,0:T(8,128)S(1)}, f32[8,8,8,1]{3,1,2,0:T(8,128)S(1)}, u32[]{:S(2)}, u32[]{:S(2)}) collective-permute-start(f32[8,8,8,1]{3,1,2,0:T(8,128)S(1)} %get-tuple-element.24), channel_id=1, source_target_pairs={{128,0},{256,128},{384,256},{0,384},{129,1},{257,129},{385,257},{1... | collective-permute-start | bytes 6152 | tf_op jit(solution)/shard_map/ppermute | solution.py:18
  77.8 16.7 %collective-permute-start.6 = (f32[8,8,1,512]{3,1,2,0:T(8,128)S(1)}, f32[8,8,1,512]{3,1,2,0:T(8,128)S(1)}, u32[]{:S(2)}, u32[]{:S(2)}) collective-permute-start(f32[8,8,1,512]{3,1,2,0:T(8,128)S(1)} %get-tuple-element.21), channel_id=1, source_target_pairs={{0,2},{2,4},{4,6},{6,8},{8,10},{10,12},{12,14},{14,16},{16,18},{18... | collective-permute-start | bytes 393224 | tf_op jit(solution)/shard_map/ppermute | solution.py:17
  79.1 16.2 %copy-start.2 = (f32[8,1,1,128]{3,2,1,0:T(1,128)S(1)}, f32[8,1,1,128]{3,2,1,0:T(1,128)}, u32[]{:S(2)}) copy-start(f32[8,1,1,128]{3,2,1,0:T(1,128)} %param.18) | copy-start | bytes 12292
  79.2 16.2 %copy-start.8 = (s32[1,1,128]{2,1,0:T(1,128)S(1)}, s32[1,1,128]{2,1,0:T(1,128)}, u32[]{:S(2)}) copy-start(s32[1,1,128]{2,1,0:T(1,128)} %param.15) | copy-start | bytes 1540
  79.2 15.4 %collective-permute-start.7 = (f32[8,8,1,512]{3,1,2,0:T(8,128)S(1)}, f32[8,8,1,512]{3,1,2,0:T(8,128)S(1)}, u32[]{:S(2)}, u32[]{:S(2)}) collective-permute-start(f32[8,8,1,512]{3,1,2,0:T(8,128)S(1)} %get-tuple-element.22), channel_id=1, source_target_pairs={{2,0},{4,2},{6,4},{8,6},{10,8},{12,10},{14,12},{16,14},{18,16},{20... | collective-permute-start | bytes 393224 | tf_op jit(solution)/shard_map/ppermute | solution.py:18
  80.6 14.0 %collective-permute-start.4 = (f32[8,8,8,1]{3,1,2,0:T(8,128)S(1)}, f32[8,8,8,1]{3,1,2,0:T(8,128)S(1)}, u32[]{:S(2)}, u32[]{:S(2)}) collective-permute-start(f32[8,8,8,1]{3,1,2,0:T(8,128)S(1)} %get-tuple-element.19), channel_id=1, source_target_pairs={{0,128},{128,256},{256,384},{384,0},{1,129},{129,257},{257,385},{3... | collective-permute-start | bytes 6152 | tf_op jit(solution)/shard_map/ppermute | solution.py:17
  82.5 12.0 %collective-permute-start.5 = (f32[8,8,8,1]{3,1,2,0:T(8,128)S(1)}, f32[8,8,8,1]{3,1,2,0:T(8,128)S(1)}, u32[]{:S(2)}, u32[]{:S(2)}) collective-permute-start(f32[8,8,8,1]{3,1,2,0:T(8,128)S(1)} %get-tuple-element.20), channel_id=1, source_target_pairs={{128,0},{256,128},{384,256},{0,384},{129,1},{257,129},{385,257},{1... | collective-permute-start | bytes 6152 | tf_op jit(solution)/shard_map/ppermute | solution.py:18
  86.5 11.3 %copy-start.3 = (f32[8,1,1,128]{3,2,1,0:T(1,128)S(1)}, f32[8,1,1,128]{3,2,1,0:T(1,128)}, u32[]{:S(2)}) copy-start(f32[8,1,1,128]{3,2,1,0:T(1,128)} %param.17) | copy-start | bytes 12292
  86.5 14.0 %copy-start.6 = (f32[1,1,128]{2,1,0:T(1,128)S(1)}, f32[1,1,128]{2,1,0:T(1,128)}, u32[]{:S(2)}) copy-start(f32[1,1,128]{2,1,0:T(1,128)} %param.19) | copy-start | bytes 1540
  86.5 14.0 %copy-start.7 = (f32[1,1,128]{2,1,0:T(1,128)S(1)}, f32[1,1,128]{2,1,0:T(1,128)}, u32[]{:S(2)}) copy-start(f32[1,1,128]{2,1,0:T(1,128)} %param.20) | copy-start | bytes 1540
  102.6 22.6 %collective-permute-start.10 = (f32[8,8,1,512]{3,1,2,0:T(8,128)S(1)}, f32[8,8,1,512]{3,1,2,0:T(8,128)S(1)}, u32[]{:S(2)}, u32[]{:S(2)}) collective-permute-start(f32[8,8,1,512]{3,1,2,0:T(8,128)S(1)} %slice.165), channel_id=1, source_target_pairs={{2,0},{4,2},{6,4},{8,6},{10,8},{12,10},{14,12},{16,14},{18,16},{20... | collective-permute-start | bytes 393224 | tf_op jit(solution)/shard_map/ppermute | solution.py:31
  103.9 21.3 %collective-permute-start.11 = (f32[8,8,1,512]{3,1,2,0:T(8,128)S(1)}, f32[8,8,1,512]{3,1,2,0:T(8,128)S(1)}, u32[]{:S(2)}, u32[]{:S(2)}) collective-permute-start(f32[8,8,1,512]{3,1,2,0:T(8,128)S(1)} %slice.166), channel_id=1, source_target_pairs={{0,2},{2,4},{4,6},{6,8},{8,10},{10,12},{12,14},{14,16},{16,18},{18... | collective-permute-start | bytes 393224 | tf_op jit(solution)/shard_map/ppermute | solution.py:31
  109.0 11.3 %collective-permute-start.8 = (f32[8,8,8,1]{3,1,2,0:T(8,128)S(1)}, f32[8,8,8,1]{3,1,2,0:T(8,128)S(1)}, u32[]{:S(2)}, u32[]{:S(2)}) collective-permute-start(f32[8,8,8,1]{3,1,2,0:T(8,128)S(1)} %slice.161), channel_id=1, source_target_pairs={{0,384},{128,0},{256,128},{384,256},{1,385},{129,1},{257,129},{385... | collective-permute-start | bytes 6152 | tf_op jit(solution)/shard_map/ppermute | solution.py:25
  110.9 14.3 %collective-permute-start.9 = (f32[8,8,8,1]{3,1,2,0:T(8,128)S(1)}, f32[8,8,8,1]{3,1,2,0:T(8,128)S(1)}, u32[]{:S(2)}, u32[]{:S(2)}) collective-permute-start(f32[8,8,8,1]{3,1,2,0:T(8,128)S(1)} %slice.162), channel_id=1, source_target_pairs={{0,128},{128,256},{256,384},{384,0},{1,129},{129,257},{257,385},{3... | collective-permute-start | bytes 6152 | tf_op jit(solution)/shard_map/ppermute | solution.py:25
  126.3 18.5 %collective-permute-start.12 = (f32[8,8,8,1]{3,1,2,0:T(8,128)S(1)}, f32[8,8,8,1]{3,1,2,0:T(8,128)S(1)}, u32[]{:S(2)}, u32[]{:S(2)}) collective-permute-start(f32[8,8,8,1]{3,1,2,0:T(8,128)S(1)} %slice.169), channel_id=1, source_target_pairs={{0,384},{128,0},{256,128},{384,256},{1,385},{129,1},{257,129},{385... | collective-permute-start | bytes 6152 | tf_op jit(solution)/shard_map/ppermute | solution.py:25
  129.7 19.0 %collective-permute-start.15 = (f32[8,8,1,512]{3,1,2,0:T(8,128)S(1)}, f32[8,8,1,512]{3,1,2,0:T(8,128)S(1)}, u32[]{:S(2)}, u32[]{:S(2)}) collective-permute-start(f32[8,8,1,512]{3,1,2,0:T(8,128)S(1)} %slice.174), channel_id=1, source_target_pairs={{0,2},{2,4},{4,6},{6,8},{8,10},{10,12},{12,14},{14,16},{16,18},{18... | collective-permute-start | bytes 393224 | tf_op jit(solution)/shard_map/ppermute | solution.py:31
  137.7 18.3 %collective-permute-start.14 = (f32[8,8,1,512]{3,1,2,0:T(8,128)S(1)}, f32[8,8,1,512]{3,1,2,0:T(8,128)S(1)}, u32[]{:S(2)}, u32[]{:S(2)}) collective-permute-start(f32[8,8,1,512]{3,1,2,0:T(8,128)S(1)} %slice.173), channel_id=1, source_target_pairs={{2,0},{4,2},{6,4},{8,6},{10,8},{12,10},{14,12},{16,14},{18,16},{20... | collective-permute-start | bytes 393224 | tf_op jit(solution)/shard_map/ppermute | solution.py:31
  139.1 9.2 collective-permute-start.13
  156.1 3.2 copy-start.5
